TPU v7x, 32 devices: a whole 2x2x4 slice. The times are simulated.
32 devices in a mesh: grp: 2 (over y), row: 4 (over z), col: 2 (over x), pair: 2 (over core).
Axes of the slice: x: 2, y: 2, z: 4, core: 2. Of those that a mesh axis runs over, the one named last changes fastest.
Arguments:
- features_in: bfloat16 [128, 32, 512], P('grp', 'row', ('col', 'pair')), parts along dimension 0, may hold values from -8 to 8
- filters_one: bfloat16 [64, 3, 3, 64], replicated, may hold values from -0.25 to 0.25
- filters_two: bfloat16 [512, 3, 3, 256], P('row'), may hold values from -0.125 to 0.125
- out_grad: bfloat16 [1024, 128, 8], P(('grp', 'row'), ('col', 'pair')), parts along dimension 0, may hold values from -24 to 24
Outputs:
- input_grad: bfloat16 [128, 32, 512], P('grp', 'row', ('col', 'pair')), parts along dimension 0
- grad_one: float32 [128, 3, 3, 64], P('grp'), parts along dimension 0
- grad_two: float32 [1024, 3, 3, 256], P(('grp', 'row')), parts along dimension 0
There are 2 independent parts, one for each index of `grp`. A program takes and returns all parts, laid end to end along the dimension named above; an argument that names none is the same for every part. Nothing has to cross between parts.
All inputs are finite; a program needn't handle non-finite values.
Results may differ from a plain program's by a relative error of at most 0.015.
Values may be sent and summed in bfloat16 or wider, within the bound.
A program may use at most 64 MiB of HBM per device.

v0:
```python
import math
import jax
import jax.numpy as jnp
from jax import lax
from jax.sharding import PartitionSpec as P


def padded_2(cells, sides, width):
    for axis, dim in sides:
        count = lax.axis_size(axis)
        ends = count - 1
        head = lax.slice_in_dim(cells, 0, width, axis=dim)
        tail = lax.slice_in_dim(cells, cells.shape[dim] - width, cells.shape[dim], axis=dim)
        cells = jnp.concatenate(
            [
                lax.ppermute(tail, axis, [(i, (i + 1) % count) for i in range(ends)]),
                cells,
                lax.ppermute(head, axis, [((i + 1) % count, i) for i in range(ends)]),
            ],
            axis=dim,
        )
    return cells


def conv_valid(padded, kernel):
    return lax.conv_general_dilated(
        padded[None],
        kernel,
        (1, 1),
        "VALID",
        dimension_numbers=("NCHW", "OHWI", "NCHW"),
        preferred_element_type=jnp.float32,
    )[0]


def flip_kernel(kernel):
    return jnp.transpose(kernel[:, ::-1, ::-1, :], (3, 1, 2, 0))


def silu_slope(values):
    sigmoid_value = jax.nn.sigmoid(values)
    return sigmoid_value * (1.0 + values * (1.0 - sigmoid_value))


def tap_grads(gradient, padded):
    row_count, col_count = (gradient.shape[1], gradient.shape[2])
    tap_list = []
    for first_tap in range(3):
        tap_row = []
        for second_tap in range(3):
            window = padded[
                :, first_tap : first_tap + row_count, second_tap : second_tap + col_count
            ]
            tap_row.append(
                jnp.einsum("ohw,chw->oc", gradient, window, preferred_element_type=jnp.float32)
            )
        tap_list.append(jnp.stack(tap_row, 1))
    return jnp.stack(tap_list, 1)


def pool_columns(active):
    channels, row_count, col_count = active.shape
    folded = active.reshape(channels, row_count // 4, 2, 2, col_count // 4, 2, 2).mean(axis=(3, 6))
    return jnp.transpose(folded, (0, 2, 4, 3, 1)).reshape(
        channels * 4, col_count // 4, row_count // 4
    )


def unpool_columns(gradient):
    quad_count, col_count, row_count = gradient.shape
    ordered = jnp.transpose(
        gradient.reshape(quad_count // 4, 2, 2, col_count, row_count), (0, 4, 1, 3, 2)
    )
    spread = (
        jnp.broadcast_to(
            ordered[:, :, :, None, :, :, None], (quad_count // 4, row_count, 2, 2, col_count, 2, 2)
        )
        * 0.25
    )
    return spread.reshape(quad_count // 4, row_count * 4, col_count * 4)


def local(features_in, filters_one, filters_two, out_grad):
    band_rows = features_in.shape[1]
    strip_cols = features_in.shape[2]
    height = band_rows * lax.axis_size("row")
    width = strip_cols * lax.axis_size(("col", "pair"))
    padded_in = padded_2(features_in, (("row", 1), (("col", "pair"), 2)), 1)
    pre_one = conv_valid(padded_in, filters_one)
    pooled = pool_columns(jax.nn.silu(pre_one)).astype(jnp.bfloat16)
    with_edges = padded_2(pooled, ((("col", "pair"), 1),), 1)
    column_strip = lax.all_gather(with_edges, "row", axis=2, tiled=True)
    strip_padded = jnp.pad(column_strip, ((0, 0), (0, 0), (1, 1)))
    swapped = jnp.transpose(filters_two, (0, 2, 1, 3))
    pre_two = conv_valid(strip_padded, swapped)
    grad_pre_two = (out_grad.astype(jnp.float32) * silu_slope(pre_two)).astype(jnp.bfloat16)
    pooled_height = column_strip.shape[2]
    pooled_width = strip_cols // 4 * lax.axis_size(("col", "pair"))
    local_two = jnp.transpose(tap_grads(grad_pre_two, strip_padded), (0, 2, 1, 3))
    grad_two = lax.psum(local_two, ("col", "pair")) / math.sqrt(pooled_height * pooled_width)
    padded_grad = jnp.pad(grad_pre_two, ((0, 0), (2, 2), (1, 1)))
    spread_grad = conv_valid(padded_grad, flip_kernel(swapped))
    with_ghosts = padded_2(spread_grad, ((("col", "pair"), 1),), 1)
    real_columns = spread_grad[:, 1:-1, :]
    real_columns = real_columns.at[:, 0, :].add(with_ghosts[:, 0, :])
    real_columns = real_columns.at[:, -1, :].add(with_ghosts[:, -1, :])
    grad_pooled = lax.psum_scatter(real_columns, "row", scatter_dimension=2, tiled=True)
    grad_pre_one = (unpool_columns(grad_pooled) * silu_slope(pre_one)).astype(jnp.bfloat16)
    local_one = tap_grads(grad_pre_one, padded_in)
    grad_one = lax.psum(local_one, ("row", "col", "pair")) / math.sqrt(height * width)
    rimmed_one = padded_2(grad_pre_one, (("row", 1), (("col", "pair"), 2)), 1)
    input_grad = conv_valid(rimmed_one, flip_kernel(filters_one)).astype(jnp.bfloat16)
    return (input_grad, grad_one, grad_two)


def solution(mesh):
    in_specs = (
        P("grp", "row", ("col", "pair")),
        P(),
        P("row", None, None, None),
        P(("grp", "row"), ("col", "pair"), None),
    )
    out_specs = (
        P("grp", "row", ("col", "pair")),
        P("grp", None, None, None),
        P(("grp", "row"), None, None, None),
    )
    return jax.shard_map(local, mesh=mesh, in_specs=in_specs, out_specs=out_specs, check_vma=False)
```

profile of v0, /device:TPU:0, one launch (start us, length us, event | category | flops | bytes accessed | tf_op | source)
XLA Modules:
  0.0 211.8 jit_solution(14888131075437018906)
XLA Ops:
  8.1 1.0 copy.216
  9.1 4.9 %collective-permute-start = (bf16[64,1,128]{2,0,1:T(8,128)(2,1)S(1)}, bf16[64,1,128]{2,0,1:T(8,128)(2,1)S(1)}, u32[]{:S(2)}, u32[]{:S(2)}) collective-permute-start(bf16[64,1,128]{2,0,1:T(8,128)(2,1)S(1)} %get-tuple-element.58), channel_id=1, source_target_pairs={{0,4},{4,8},{8,12},{1,5},{5,9},{9,13},{2,6},{6,10},{10,14},{3,7},{... | collective-permute-start | bytes 49160 | tf_op jit(solution)/shard_map/ppermute | solution.py:16
  14.0 1.3 collective-permute-start.1
  15.4 0.9 constant_dynamic-update-slice_fusion.1
  16.4 3.3 %collective-permute-done.1 = bf16[64,1,128]{2,0,1:T(8,128)(2,1)S(1)} collective-permute-done((bf16[64,1,128]{2,0,1:T(8,128)(2,1)S(1)}, bf16[64,1,128]{2,0,1:T(8,128)(2,1)S(1)}, u32[]{:S(2)}, u32[]{:S(2)}) %collective-permute-start.1) | collective-permute-done | bytes 16416 | tf_op jit(solution)/shard_map/ppermute | solution.py:18
  19.7 1.3 collective-permute-start.3
  21.0 3.0 %collective-permute-start.2 = (bf16[64,10,1]{2,0,1:T(8,128)(2,1)S(1)}, bf16[64,10,1]{2,0,1:T(8,128)(2,1)S(1)}, u32[]{:S(2)}, u32[]{:S(2)}) collective-permute-start(bf16[64,10,1]{2,0,1:T(8,128)(2,1)S(1)} %get-tuple-element.51), channel_id=1, source_target_pairs={{0,1},{1,2},{2,3},{4,5},{5,6},{6,7},{8,9},{9,10},{10,11},{12,13},{... | collective-permute-start | bytes 3848 | tf_op jit(solution)/shard_map/ppermute | solution.py:16
  24.1 1.0 collective-permute-done.2
  25.3 0.3 copy.265
  25.9 0.6 copy-done.3
  26.5 0.8 convolution_select_fusion.1
  27.6 0.9 fusion.3
  28.8 1.3 collective-permute-start.5
  30.1 4.9 %collective-permute-start.4 = (bf16[256,1,2]{1,0,2:T(8,128)(2,1)S(1)}, bf16[256,1,2]{1,0,2:T(8,128)(2,1)S(1)}, u32[]{:S(2)}, u32[]{:S(2)}) collective-permute-start(bf16[256,1,2]{1,0,2:T(8,128)(2,1)S(1)} %get-tuple-element.55), channel_id=1, source_target_pairs={{0,1},{1,2},{2,3},{4,5},{5,6},{6,7},{8,9},{9,10},{10,11},{12,13},{... | collective-permute-start | bytes 3080 | tf_op jit(solution)/shard_map/ppermute | solution.py:16
  35.0 0.2 copy.264
  35.3 0.7 collective-permute-done.4
  36.2 13.7 %all_gather.3 = bf16[256,34,8]{0,1,2:T(8,128)(2,1)S(1)} all-gather(bf16[256,34,2]{0,1,2:T(8,128)(2,1)S(1)} %copy.226), channel_id=1, replica_groups=mesh['grp'=2,'row'=4,'col'=2,'pair'=2] {'row'}, dimensions={2}, use_global_device_ids=true | all-gather | bytes 174080 | tf_op jit(solution)/shard_map/all_gather | solution.py:92
  50.1 1.0 fusion.6
  52.8 1.0 fusion.4
  53.9 2.4 %collective-permute-start.6 = (f32[256,1,8]{0,2,1:T(8,128)S(1)}, f32[256,1,8]{0,2,1:T(8,128)S(1)}, u32[]{:S(2)}, u32[]{:S(2)}) collective-permute-start(f32[256,1,8]{0,2,1:T(8,128)S(1)} %get-tuple-element.48), channel_id=1, source_target_pairs={{0,1},{1,2},{2,3},{4,5},{5,6},{6,7},{8,9},{9,10},{10,11},{12,13},{... | collective-permute-start | bytes 24584 | tf_op jit(solution)/shard_map/ppermute | solution.py:16
  56.6 1.3 collective-permute-start.7
  57.9 6.6 %collective-permute-done.7 = f32[256,1,8]{0,2,1:T(8,128)S(1)} collective-permute-done((f32[256,1,8]{0,2,1:T(8,128)S(1)}, f32[256,1,8]{0,2,1:T(8,128)S(1)}, u32[]{:S(2)}, u32[]{:S(2)}) %collective-permute-start.7) | collective-permute-done | bytes 8224 | tf_op jit(solution)/shard_map/ppermute | solution.py:18
  64.4 0.8 copy.233
  65.7 1.1 maximum_bitcast_fusion
  66.8 18.7 %reduce-scatter.2.cloned.1.call-done = f32[256,32,2]{0,1,2:T(8,128)} async-done(((f32[256,32,8]{0,1,2:T(8,128)}), f32[256,32,2]{0,1,2:T(8,128)}) %reduce-scatter.2.cloned.1.call-update) | async-done | bytes 65552 | tf_op jit(solution)/shard_map/reduce_scatter | solution.py:107
  85.5 0.8 broadcast_multiply_fusion.2
  87.1 0.4 copy-done.1
  87.7 1.3 collective-permute-start.8
  89.0 1.3 collective-permute-start.9
  90.3 0.3 convolution_bitcast_fusion.15
  90.8 0.3 convolution_bitcast_fusion.17
  91.0 0.3 convolution_bitcast_fusion.12
  91.3 0.3 convolution_bitcast_fusion.14
  91.6 0.3 convolution_bitcast_fusion.9
  92.0 0.2 convolution_bitcast_fusion.11
  92.4 2.4 %collective-permute-done.9 = bf16[64,1,128]{2,1,0:T(2,128)(2,1)S(1)} collective-permute-done((bf16[64,1,128]{2,1,0:T(2,128)(2,1)S(1)}, bf16[64,1,128]{2,1,0:T(2,128)(2,1)S(1)}, u32[]{:S(2)}, u32[]{:S(2)}) %collective-permute-start.9) | collective-permute-done | bytes 16416 | tf_op jit(solution)/shard_map/ppermute | solution.py:18
  94.9 1.3 collective-permute-start.11
  96.2 3.0 %collective-permute-start.10 = (bf16[64,10,1]{2,0,1:T(8,128)(2,1)S(1)}, bf16[64,10,1]{2,0,1:T(8,128)(2,1)S(1)}, u32[]{:S(2)}, u32[]{:S(2)}) collective-permute-start(bf16[64,10,1]{2,0,1:T(8,128)(2,1)S(1)} %get-tuple-element.49), channel_id=1, source_target_pairs={{0,1},{1,2},{2,3},{4,5},{5,6},{6,7},{8,9},{9,10},{10,11},{12,13},{... | collective-permute-start | bytes 3848 | tf_op jit(solution)/shard_map/ppermute | solution.py:16
  99.3 0.7 pad_maximum_fusion
  100.0 0.2 collective-permute-done.10
  100.5 0.3 copy.266
  101.0 0.6 fusion
  101.7 0.9 copy.259
  102.6 5.7 %all-reduce.7.cloned.1.call-done = f32[128,3,3,256]{3,0,1,2:T(8,128)} async-done(((f32[128,3,3,256]{3,0,1,2:T(8,128)}), f32[128,3,3,256]{3,0,1,2:T(8,128)}) %all-reduce.7.cloned.1.call-update) | async-done | bytes 1179664 | tf_op jit(solution)/shard_map/psum | solution.py:100
  108.3 1.4 broadcast_multiply_fusion
  109.7 1.1 copy.260
  110.8 91.9 %all-reduce.5.cloned.1.call-done = f32[64,3,3,64]{3,0,2,1:T(8,128)} async-done(((f32[64,3,3,64]{3,0,2,1:T(8,128)}), f32[64,3,3,64]{3,0,2,1:T(8,128)}) %all-reduce.5.cloned.1.call-update) | async-done | bytes 147472 | tf_op jit(solution)/shard_map/psum | solution.py:110
  202.6 1.7 broadcast_multiply_fusion.1
  (79 shorter events, 6.1 us)
Async XLA Ops:
  8.0 42.1 %copy-start = (bf16[128,3,3,256]{3,0,2,1:T(8,128)(2,1)S(1)}, bf16[128,3,3,256]{3,0,2,1:T(8,128)(2,1)}, u32[]{:S(2)}) copy-start(bf16[128,3,3,256]{3,0,2,1:T(8,128)(2,1)} %param.10) | copy-start | bytes 1769476
  8.0 77.5 %reduce-scatter.2.cloned.1.call-start = ((), (), s32[]{:S(2)}) async-start(), calls=%async_computation.1 | async-start | bytes 327680 | tf_op jit(solution)/shard_map/reduce_scatter | solution.py:107
  9.1 6.4 %collective-permute-start = (bf16[64,1,128]{2,0,1:T(8,128)(2,1)S(1)}, bf16[64,1,128]{2,0,1:T(8,128)(2,1)S(1)}, u32[]{:S(2)}, u32[]{:S(2)}) collective-permute-start(bf16[64,1,128]{2,0,1:T(8,128)(2,1)S(1)} %get-tuple-element.58), channel_id=1, source_target_pairs={{0,4},{4,8},{8,12},{1,5},{5,9},{9,13},{2,6},{6,10},{10,14},{3,7},{... | collective-permute-start | bytes 49160 | tf_op jit(solution)/shard_map/ppermute | solution.py:16
  14.0 5.6 %collective-permute-start.1 = (bf16[64,1,128]{2,0,1:T(8,128)(2,1)S(1)}, bf16[64,1,128]{2,0,1:T(8,128)(2,1)S(1)}, u32[]{:S(2)}, u32[]{:S(2)}) collective-permute-start(bf16[64,1,128]{2,0,1:T(8,128)(2,1)S(1)} %get-tuple-element.57), channel_id=1, source_target_pairs={{4,0},{8,4},{12,8},{5,1},{9,5},{13,9},{6,2},{10,6},{14,10},{7,3},{... | collective-permute-start | bytes 49160 | tf_op jit(solution)/shard_map/ppermute | solution.py:18
  19.7 4.4 %collective-permute-start.3 = (bf16[64,10,1]{2,0,1:T(8,128)(2,1)S(1)}, bf16[64,10,1]{2,0,1:T(8,128)(2,1)S(1)}, u32[]{:S(2)}, u32[]{:S(2)}) collective-permute-start(bf16[64,10,1]{2,0,1:T(8,128)(2,1)S(1)} %get-tuple-element.52), channel_id=1, source_target_pairs={{1,0},{2,1},{3,2},{5,4},{6,5},{7,6},{9,8},{10,9},{11,10},{13,12},{... | collective-permute-start | bytes 3848 | tf_op jit(solution)/shard_map/ppermute | solution.py:18
  21.0 4.0 %collective-permute-start.2 = (bf16[64,10,1]{2,0,1:T(8,128)(2,1)S(1)}, bf16[64,10,1]{2,0,1:T(8,128)(2,1)S(1)}, u32[]{:S(2)}, u32[]{:S(2)}) collective-permute-start(bf16[64,10,1]{2,0,1:T(8,128)(2,1)S(1)} %get-tuple-element.51), channel_id=1, source_target_pairs={{0,1},{1,2},{2,3},{4,5},{5,6},{6,7},{8,9},{9,10},{10,11},{12,13},{... | collective-permute-start | bytes 3848 | tf_op jit(solution)/shard_map/ppermute | solution.py:16
  25.6 0.9 copy-start.3
  25.6 0.9 copy-start.4
  28.8 6.4 %collective-permute-start.5 = (bf16[256,1,2]{1,0,2:T(8,128)(2,1)S(1)}, bf16[256,1,2]{1,0,2:T(8,128)(2,1)S(1)}, u32[]{:S(2)}, u32[]{:S(2)}) collective-permute-start(bf16[256,1,2]{1,0,2:T(8,128)(2,1)S(1)} %get-tuple-element.56), channel_id=1, source_target_pairs={{1,0},{2,1},{3,2},{5,4},{6,5},{7,6},{9,8},{10,9},{11,10},{13,12},{... | collective-permute-start | bytes 3080 | tf_op jit(solution)/shard_map/ppermute | solution.py:18
  30.1 5.9 %collective-permute-start.4 = (bf16[256,1,2]{1,0,2:T(8,128)(2,1)S(1)}, bf16[256,1,2]{1,0,2:T(8,128)(2,1)S(1)}, u32[]{:S(2)}, u32[]{:S(2)}) collective-permute-start(bf16[256,1,2]{1,0,2:T(8,128)(2,1)S(1)} %get-tuple-element.55), channel_id=1, source_target_pairs={{0,1},{1,2},{2,3},{4,5},{5,6},{6,7},{8,9},{9,10},{10,11},{12,13},{... | collective-permute-start | bytes 3080 | tf_op jit(solution)/shard_map/ppermute | solution.py:16
  50.1 1.0 copy-start.2
  53.9 4.0 %collective-permute-start.6 = (f32[256,1,8]{0,2,1:T(8,128)S(1)}, f32[256,1,8]{0,2,1:T(8,128)S(1)}, u32[]{:S(2)}, u32[]{:S(2)}) collective-permute-start(f32[256,1,8]{0,2,1:T(8,128)S(1)} %get-tuple-element.48), channel_id=1, source_target_pairs={{0,1},{1,2},{2,3},{4,5},{5,6},{6,7},{8,9},{9,10},{10,11},{12,13},{... | collective-permute-start | bytes 24584 | tf_op jit(solution)/shard_map/ppermute | solution.py:16
  56.6 7.9 %collective-permute-start.7 = (f32[256,1,8]{0,2,1:T(8,128)S(1)}, f32[256,1,8]{0,2,1:T(8,128)S(1)}, u32[]{:S(2)}, u32[]{:S(2)}) collective-permute-start(f32[256,1,8]{0,2,1:T(8,128)S(1)} %get-tuple-element.47), channel_id=1, source_target_pairs={{1,0},{2,1},{3,2},{5,4},{6,5},{7,6},{9,8},{10,9},{11,10},{13,12},{... | collective-permute-start | bytes 24584 | tf_op jit(solution)/shard_map/ppermute | solution.py:18
  65.3 43.0 %all-reduce.7.cloned.1.call-start = ((), (), s32[]{:S(2)}) async-start(), calls=%async_computation.3 | async-start | bytes 2359296 | tf_op jit(solution)/shard_map/psum | solution.py:100
  66.8 135.9 %all-reduce.5.cloned.1.call-start = ((), (), s32[]{:S(2)}) async-start(), calls=%async_computation.2 | async-start | bytes 589824 | tf_op jit(solution)/shard_map/psum | solution.py:110
  86.6 0.9 copy-start.1
  87.7 4.6 %collective-permute-start.8 = (bf16[64,1,128]{2,1,0:T(2,128)(2,1)S(1)}, bf16[64,1,128]{2,1,0:T(2,128)(2,1)S(1)}, u32[]{:S(2)}, u32[]{:S(2)}) collective-permute-start(bf16[64,1,128]{2,1,0:T(2,128)(2,1)S(1)} %get-tuple-element.54), channel_id=1, source_target_pairs={{0,4},{4,8},{8,12},{1,5},{5,9},{9,13},{2,6},{6,10},{10,14},{3,7},{... | collective-permute-start | bytes 49160 | tf_op jit(solution)/shard_map/ppermute | solution.py:16
  89.0 5.8 %collective-permute-start.9 = (bf16[64,1,128]{2,1,0:T(2,128)(2,1)S(1)}, bf16[64,1,128]{2,1,0:T(2,128)(2,1)S(1)}, u32[]{:S(2)}, u32[]{:S(2)}) collective-permute-start(bf16[64,1,128]{2,1,0:T(2,128)(2,1)S(1)} %get-tuple-element.53), channel_id=1, source_target_pairs={{4,0},{8,4},{12,8},{5,1},{9,5},{13,9},{6,2},{10,6},{14,10},{7,3},{... | collective-permute-start | bytes 49160 | tf_op jit(solution)/shard_map/ppermute | solution.py:18
  94.9 5.1 %collective-permute-start.11 = (bf16[64,10,1]{2,0,1:T(8,128)(2,1)S(1)}, bf16[64,10,1]{2,0,1:T(8,128)(2,1)S(1)}, u32[]{:S(2)}, u32[]{:S(2)}) collective-permute-start(bf16[64,10,1]{2,0,1:T(8,128)(2,1)S(1)} %get-tuple-element.50), channel_id=1, source_target_pairs={{1,0},{2,1},{3,2},{5,4},{6,5},{7,6},{9,8},{10,9},{11,10},{13,12},{... | collective-permute-start | bytes 3848 | tf_op jit(solution)/shard_map/ppermute | solution.py:18
  96.2 4.0 %collective-permute-start.10 = (bf16[64,10,1]{2,0,1:T(8,128)(2,1)S(1)}, bf16[64,10,1]{2,0,1:T(8,128)(2,1)S(1)}, u32[]{:S(2)}, u32[]{:S(2)}) collective-permute-start(bf16[64,10,1]{2,0,1:T(8,128)(2,1)S(1)} %get-tuple-element.49), channel_id=1, source_target_pairs={{0,1},{1,2},{2,3},{4,5},{5,6},{6,7},{8,9},{9,10},{10,11},{12,13},{... | collective-permute-start | bytes 3848 | tf_op jit(solution)/shard_map/ppermute | solution.py:16
Sparse Core Ops, SparseCore 0:
  65.4 20.0 reduce-scatter.1
Sparse Core Ops, SparseCore 1:
  68.8 39.4 all-reduce.6
  112.5 90.1 all-reduce.4
where the time goes:
time: 212 us
  waiting for transfers between devices  131 us (62%)
  starting transfers between devices  27.5 us (13%)
  between operations  16.1 us (8%)
  blocking collectives  13.7 us (6%)
  local copies, waits for them, and re-layouts  8.75 us (4%)
  other arithmetic  7.58 us (4%)
  matrix products  7.49 us (4%)
    psum x1, waiting for transfers between devices, local(): lax.psum(local_one, ('row', 'col', 'pair')) / math.sqrt(height * width)  91.9 us
    ppermute x6, starting transfers between devices, padded_2(): lax.ppermute(tail, axis, [(i, (i + 1) % count) for i in range(ends)])  19.6 us
    reduce_scatter x1, waiting for transfers between devices, local(): lax.psum_scatter(real_columns, 'row', scatter_dimension=2, tiled=True)  18.7 us
    all_gather x1, blocking collectives, local(): column_strip = lax.all_gather(with_edges, 'row', axis=2, tiled=True)  13.7 us
    ppermute x6, waiting for transfers between devices, padded_2(): lax.ppermute(head, axis, [((i + 1) % count, i) for i in range(ends)])  12.2 us
    ppermute x6, starting transfers between devices, padded_2(): lax.ppermute(head, axis, [((i + 1) % count, i) for i in range(ends)])  7.75 us
    psum x1, waiting for transfers between devices, local(): lax.psum(local_two, ('col', 'pair'))  5.73 us
    unnamed x21, local copies, waits for them, and re-layouts  5.7 us
  transfers between devices with their start and end apart: 15, of which 10 were waited for; matrix products, arithmetic and copies ran while one was open for 6% of the time, Pallas kernels for 0%

commit v1 on v0

--- a/solution.py
+++ b/solution.py
@@ -3,6 +3,10 @@
 import jax.numpy as jnp
 from jax import lax
 from jax.sharding import PartitionSpec as P
+
+keep_up_shards_over_axis = lambda shard_in, along_axis, mesh_ax: lax.psum(
+    lax.psum(shard_in, axis_name=along_axis), axis_name=mesh_ax
+)
 
 
 def padded_2(cells, sides, width):
@@ -107,7 +111,9 @@
     grad_pooled = lax.psum_scatter(real_columns, "row", scatter_dimension=2, tiled=True)
     grad_pre_one = (unpool_columns(grad_pooled) * silu_slope(pre_one)).astype(jnp.bfloat16)
     local_one = tap_grads(grad_pre_one, padded_in)
-    grad_one = lax.psum(local_one, ("row", "col", "pair")) / math.sqrt(height * width)
+    grad_one = keep_up_shards_over_axis(local_one, ("col", "pair"), "row") / math.sqrt(
+        height * width
+    )
     rimmed_one = padded_2(grad_pre_one, (("row", 1), (("col", "pair"), 2)), 1)
     input_grad = conv_valid(rimmed_one, flip_kernel(filters_one)).astype(jnp.bfloat16)
     return (input_grad, grad_one, grad_two)

time: 212 us -> 184 us (0.87)
  waiting for transfers between devices: 131 us -> 104 us
    psum x2, waiting for transfers between devices: 97.6 us -> 70.4 us  [the longest x1 35.8 us: lax.psum(lax.psum(shard_in, axis_name=along_axis), axis_name=mesh_ax)]
where the time goes in v1:
time: 184 us; the launch traced here: 183 us
  waiting for transfers between devices  104 us (57%)
  starting transfers between devices  27.5 us (15%)
  between operations  14.4 us (8%)
  blocking collectives  13.7 us (7%)
  local copies, waits for them, and re-layouts  8.75 us (5%)
  other arithmetic  7.59 us (4%)
  matrix products  7.48 us (4%)
    psum x1, waiting for transfers between devices, lax.psum(lax.psum(shard_in, axis_name=along_axis), axis_name=mesh_ax)  35.8 us
    psum x1, waiting for transfers between devices, lax.psum(shard_in, axis_name=along_axis)  34.5 us
    ppermute x6, starting transfers between devices, padded_2(): lax.ppermute(tail, axis, [(i, (i + 1) % count) for i in range(ends)])  19.6 us
    reduce_scatter x1, waiting for transfers between devices, local(): lax.psum_scatter(real_columns, 'row', scatter_dimension=2, tiled=True)  18.8 us
    all_gather x1, blocking collectives, local(): column_strip = lax.all_gather(with_edges, 'row', axis=2, tiled=True)  13.7 us
    ppermute x6, waiting for transfers between devices, padded_2(): lax.ppermute(head, axis, [((i + 1) % count, i) for i in range(ends)])  11.4 us
    ppermute x6, starting transfers between devices, padded_2(): lax.ppermute(head, axis, [((i + 1) % count, i) for i in range(ends)])  7.75 us
    unnamed x21, local copies, waits for them, and re-layouts  5.7 us
  transfers between devices with their start and end apart: 15, of which 10 were waited for; matrix products, arithmetic and copies ran while one was open for 6% of the time, Pallas kernels for 0%

profile of v1, /device:TPU:0, one launch (start us, length us, event | category | flops | bytes accessed | tf_op | source)
XLA Modules:
  0.0 183.0 jit_solution(10919358876482067859)
XLA Ops:
  7.2 1.0 copy.216
  8.2 4.9 %collective-permute-start = (bf16[64,1,128]{2,0,1:T(8,128)(2,1)S(1)}, bf16[64,1,128]{2,0,1:T(8,128)(2,1)S(1)}, u32[]{:S(2)}, u32[]{:S(2)}) collective-permute-start(bf16[64,1,128]{2,0,1:T(8,128)(2,1)S(1)} %get-tuple-element.60), channel_id=1, source_target_pairs={{0,4},{4,8},{8,12},{1,5},{5,9},{9,13},{2,6},{6,10},{10,14},{3,7},{... | collective-permute-start | bytes 49160 | tf_op jit(solution)/shard_map/ppermute | solution.py:20
  13.2 1.3 collective-permute-start.1
  14.6 0.9 constant_dynamic-update-slice_fusion.1
  15.5 3.3 %collective-permute-done.1 = bf16[64,1,128]{2,0,1:T(8,128)(2,1)S(1)} collective-permute-done((bf16[64,1,128]{2,0,1:T(8,128)(2,1)S(1)}, bf16[64,1,128]{2,0,1:T(8,128)(2,1)S(1)}, u32[]{:S(2)}, u32[]{:S(2)}) %collective-permute-start.1) | collective-permute-done | bytes 16416 | tf_op jit(solution)/shard_map/ppermute | solution.py:22
  18.9 1.3 collective-permute-start.3
  20.2 3.0 %collective-permute-start.2 = (bf16[64,10,1]{2,0,1:T(8,128)(2,1)S(1)}, bf16[64,10,1]{2,0,1:T(8,128)(2,1)S(1)}, u32[]{:S(2)}, u32[]{:S(2)}) collective-permute-start(bf16[64,10,1]{2,0,1:T(8,128)(2,1)S(1)} %get-tuple-element.53), channel_id=1, source_target_pairs={{0,1},{1,2},{2,3},{4,5},{5,6},{6,7},{8,9},{9,10},{10,11},{12,13},{... | collective-permute-start | bytes 3848 | tf_op jit(solution)/shard_map/ppermute | solution.py:20
  23.3 1.0 collective-permute-done.2
  24.5 0.3 copy.265
  25.1 0.6 copy-done.3
  25.7 0.8 convolution_select_fusion.1
  26.8 0.9 fusion.3
  28.0 1.3 collective-permute-start.5
  29.3 4.9 %collective-permute-start.4 = (bf16[256,1,2]{1,0,2:T(8,128)(2,1)S(1)}, bf16[256,1,2]{1,0,2:T(8,128)(2,1)S(1)}, u32[]{:S(2)}, u32[]{:S(2)}) collective-permute-start(bf16[256,1,2]{1,0,2:T(8,128)(2,1)S(1)} %get-tuple-element.57), channel_id=1, source_target_pairs={{0,1},{1,2},{2,3},{4,5},{5,6},{6,7},{8,9},{9,10},{10,11},{12,13},{... | collective-permute-start | bytes 3080 | tf_op jit(solution)/shard_map/ppermute | solution.py:20
  34.2 0.2 copy.264
  34.4 0.7 collective-permute-done.4
  35.4 13.7 %all_gather.3 = bf16[256,34,8]{0,1,2:T(8,128)(2,1)S(1)} all-gather(bf16[256,34,2]{0,1,2:T(8,128)(2,1)S(1)} %copy.226), channel_id=1, replica_groups=mesh['grp'=2,'row'=4,'col'=2,'pair'=2] {'row'}, dimensions={2}, use_global_device_ids=true | all-gather | bytes 174080 | tf_op jit(solution)/shard_map/all_gather | solution.py:96
  49.3 1.0 fusion.6
  52.0 1.0 fusion.4
  53.0 2.4 %collective-permute-start.6 = (f32[256,1,8]{0,2,1:T(8,128)S(1)}, f32[256,1,8]{0,2,1:T(8,128)S(1)}, u32[]{:S(2)}, u32[]{:S(2)}) collective-permute-start(f32[256,1,8]{0,2,1:T(8,128)S(1)} %get-tuple-element.50), channel_id=1, source_target_pairs={{0,1},{1,2},{2,3},{4,5},{5,6},{6,7},{8,9},{9,10},{10,11},{12,13},{... | collective-permute-start | bytes 24584 | tf_op jit(solution)/shard_map/ppermute | solution.py:20
  55.7 1.3 collective-permute-start.7
  57.0 6.6 %collective-permute-done.7 = f32[256,1,8]{0,2,1:T(8,128)S(1)} collective-permute-done((f32[256,1,8]{0,2,1:T(8,128)S(1)}, f32[256,1,8]{0,2,1:T(8,128)S(1)}, u32[]{:S(2)}, u32[]{:S(2)}) %collective-permute-start.7) | collective-permute-done | bytes 8224 | tf_op jit(solution)/shard_map/ppermute | solution.py:22
  63.6 0.8 copy.233
  64.8 1.1 maximum_bitcast_fusion
  65.9 18.8 %reduce-scatter.2.cloned.1.call-done = f32[256,32,2]{0,1,2:T(8,128)} async-done(((f32[256,32,8]{0,1,2:T(8,128)}), f32[256,32,2]{0,1,2:T(8,128)}) %reduce-scatter.2.cloned.1.call-update) | async-done | bytes 65552 | tf_op jit(solution)/shard_map/reduce_scatter | solution.py:111
  84.7 0.8 broadcast_multiply_fusion.2
  86.4 0.4 copy-done.1
  86.9 1.3 collective-permute-start.8
  88.2 1.3 collective-permute-start.9
  89.5 0.3 convolution_bitcast_fusion.9
  90.0 0.2 convolution_bitcast_fusion.11
  90.3 0.3 convolution_bitcast_fusion.15
  90.7 0.2 convolution_bitcast_fusion.17
  91.0 0.3 convolution_bitcast_fusion.12
  91.3 0.3 convolution_bitcast_fusion.14
  91.6 0.7 pad_maximum_fusion
  92.4 1.6 collective-permute-done.9
  94.2 1.3 collective-permute-start.11
  95.5 3.0 %collective-permute-start.10 = (bf16[64,10,1]{2,0,1:T(8,128)(2,1)S(1)}, bf16[64,10,1]{2,0,1:T(8,128)(2,1)S(1)}, u32[]{:S(2)}, u32[]{:S(2)}) collective-permute-start(bf16[64,10,1]{2,0,1:T(8,128)(2,1)S(1)} %get-tuple-element.51), channel_id=1, source_target_pairs={{0,1},{1,2},{2,3},{4,5},{5,6},{6,7},{8,9},{9,10},{10,11},{12,13},{... | collective-permute-start | bytes 3848 | tf_op jit(solution)/shard_map/ppermute | solution.py:20
  98.5 1.2 collective-permute-done.10
  99.9 0.3 copy.266
  100.4 0.6 fusion
  101.1 0.9 copy.259
  102.0 34.5 %all-reduce.8.cloned.1.call-done = (f32[64,3,3,64]{3,0,2,1:T(8,128)}, f32[128,3,3,256]{3,0,1,2:T(8,128)}) async-done(((f32[64,3,3,64]{3,0,2,1:T(8,128)}, f32[128,3,3,256]{3,0,1,2:T(8,128)}), (f32[64,3,3,64]{3,0,2,1:T(8,128)}, f32[128,3,3,256]{3,0,1,2:T(8,128)})) %all-reduce.8.cloned.1.call-update) | async-done | bytes 1327120 | tf_op jit(solution)/shard_map/psum | solution.py:8
  136.5 1.4 broadcast_multiply_fusion
  137.9 1.1 copy.260
  139.0 35.8 %all-reduce.6.cloned.1.call-done = f32[64,3,3,64]{3,0,2,1:T(8,128)} async-done(((f32[64,3,3,64]{3,0,2,1:T(8,128)}), f32[64,3,3,64]{3,0,2,1:T(8,128)}) %all-reduce.6.cloned.1.call-update) | async-done | bytes 147472 | tf_op jit(solution)/shard_map/psum | solution.py:7
  174.8 1.7 broadcast_multiply_fusion.1
  (79 shorter events, 6.1 us)
Async XLA Ops:
  7.2 42.1 %copy-start = (bf16[128,3,3,256]{3,0,2,1:T(8,128)(2,1)S(1)}, bf16[128,3,3,256]{3,0,2,1:T(8,128)(2,1)}, u32[]{:S(2)}) copy-start(bf16[128,3,3,256]{3,0,2,1:T(8,128)(2,1)} %param.10) | copy-start | bytes 1769476
  7.2 77.5 %reduce-scatter.2.cloned.1.call-start = ((), (), s32[]{:S(2)}) async-start(), calls=%async_computation.1 | async-start | bytes 327680 | tf_op jit(solution)/shard_map/reduce_scatter | solution.py:111
  8.2 6.4 %collective-permute-start = (bf16[64,1,128]{2,0,1:T(8,128)(2,1)S(1)}, bf16[64,1,128]{2,0,1:T(8,128)(2,1)S(1)}, u32[]{:S(2)}, u32[]{:S(2)}) collective-permute-start(bf16[64,1,128]{2,0,1:T(8,128)(2,1)S(1)} %get-tuple-element.60), channel_id=1, source_target_pairs={{0,4},{4,8},{8,12},{1,5},{5,9},{9,13},{2,6},{6,10},{10,14},{3,7},{... | collective-permute-start | bytes 49160 | tf_op jit(solution)/shard_map/ppermute | solution.py:20
  13.2 5.6 %collective-permute-start.1 = (bf16[64,1,128]{2,0,1:T(8,128)(2,1)S(1)}, bf16[64,1,128]{2,0,1:T(8,128)(2,1)S(1)}, u32[]{:S(2)}, u32[]{:S(2)}) collective-permute-start(bf16[64,1,128]{2,0,1:T(8,128)(2,1)S(1)} %get-tuple-element.59), channel_id=1, source_target_pairs={{4,0},{8,4},{12,8},{5,1},{9,5},{13,9},{6,2},{10,6},{14,10},{7,3},{... | collective-permute-start | bytes 49160 | tf_op jit(solution)/shard_map/ppermute | solution.py:22
  18.9 4.4 %collective-permute-start.3 = (bf16[64,10,1]{2,0,1:T(8,128)(2,1)S(1)}, bf16[64,10,1]{2,0,1:T(8,128)(2,1)S(1)}, u32[]{:S(2)}, u32[]{:S(2)}) collective-permute-start(bf16[64,10,1]{2,0,1:T(8,128)(2,1)S(1)} %get-tuple-element.54), channel_id=1, source_target_pairs={{1,0},{2,1},{3,2},{5,4},{6,5},{7,6},{9,8},{10,9},{11,10},{13,12},{... | collective-permute-start | bytes 3848 | tf_op jit(solution)/shard_map/ppermute | solution.py:22
  20.2 4.0 %collective-permute-start.2 = (bf16[64,10,1]{2,0,1:T(8,128)(2,1)S(1)}, bf16[64,10,1]{2,0,1:T(8,128)(2,1)S(1)}, u32[]{:S(2)}, u32[]{:S(2)}) collective-permute-start(bf16[64,10,1]{2,0,1:T(8,128)(2,1)S(1)} %get-tuple-element.53), channel_id=1, source_target_pairs={{0,1},{1,2},{2,3},{4,5},{5,6},{6,7},{8,9},{9,10},{10,11},{12,13},{... | collective-permute-start | bytes 3848 | tf_op jit(solution)/shard_map/ppermute | solution.py:20
  24.7 0.9 copy-start.3
  24.8 0.9 copy-start.4
  28.0 6.4 %collective-permute-start.5 = (bf16[256,1,2]{1,0,2:T(8,128)(2,1)S(1)}, bf16[256,1,2]{1,0,2:T(8,128)(2,1)S(1)}, u32[]{:S(2)}, u32[]{:S(2)}) collective-permute-start(bf16[256,1,2]{1,0,2:T(8,128)(2,1)S(1)} %get-tuple-element.58), channel_id=1, source_target_pairs={{1,0},{2,1},{3,2},{5,4},{6,5},{7,6},{9,8},{10,9},{11,10},{13,12},{... | collective-permute-start | bytes 3080 | tf_op jit(solution)/shard_map/ppermute | solution.py:22
  29.3 5.8 %collective-permute-start.4 = (bf16[256,1,2]{1,0,2:T(8,128)(2,1)S(1)}, bf16[256,1,2]{1,0,2:T(8,128)(2,1)S(1)}, u32[]{:S(2)}, u32[]{:S(2)}) collective-permute-start(bf16[256,1,2]{1,0,2:T(8,128)(2,1)S(1)} %get-tuple-element.57), channel_id=1, source_target_pairs={{0,1},{1,2},{2,3},{4,5},{5,6},{6,7},{8,9},{9,10},{10,11},{12,13},{... | collective-permute-start | bytes 3080 | tf_op jit(solution)/shard_map/ppermute | solution.py:20
  49.2 1.0 copy-start.2
  53.0 4.0 %collective-permute-start.6 = (f32[256,1,8]{0,2,1:T(8,128)S(1)}, f32[256,1,8]{0,2,1:T(8,128)S(1)}, u32[]{:S(2)}, u32[]{:S(2)}) collective-permute-start(f32[256,1,8]{0,2,1:T(8,128)S(1)} %get-tuple-element.50), channel_id=1, source_target_pairs={{0,1},{1,2},{2,3},{4,5},{5,6},{6,7},{8,9},{9,10},{10,11},{12,13},{... | collective-permute-start | bytes 24584 | tf_op jit(solution)/shard_map/ppermute | solution.py:20
  55.7 7.9 %collective-permute-start.7 = (f32[256,1,8]{0,2,1:T(8,128)S(1)}, f32[256,1,8]{0,2,1:T(8,128)S(1)}, u32[]{:S(2)}, u32[]{:S(2)}) collective-permute-start(f32[256,1,8]{0,2,1:T(8,128)S(1)} %get-tuple-element.49), channel_id=1, source_target_pairs={{1,0},{2,1},{3,2},{5,4},{6,5},{7,6},{9,8},{10,9},{11,10},{13,12},{... | collective-permute-start | bytes 24584 | tf_op jit(solution)/shard_map/ppermute | solution.py:22
  64.4 72.1 %all-reduce.8.cloned.1.call-start = ((), (), s32[]{:S(2)}) async-start(), calls=%async_computation.3 | async-start | bytes 2949120 | tf_op jit(solution)/shard_map/psum | solution.py:8
  85.8 0.9 copy-start.1
  86.9 5.5 %collective-permute-start.8 = (bf16[64,1,128]{2,1,0:T(2,128)(2,1)S(1)}, bf16[64,1,128]{2,1,0:T(2,128)(2,1)S(1)}, u32[]{:S(2)}, u32[]{:S(2)}) collective-permute-start(bf16[64,1,128]{2,1,0:T(2,128)(2,1)S(1)} %get-tuple-element.56), channel_id=1, source_target_pairs={{0,4},{4,8},{8,12},{1,5},{5,9},{9,13},{2,6},{6,10},{10,14},{3,7},{... | collective-permute-start | bytes 49160 | tf_op jit(solution)/shard_map/ppermute | solution.py:20
  88.2 5.8 %collective-permute-start.9 = (bf16[64,1,128]{2,1,0:T(2,128)(2,1)S(1)}, bf16[64,1,128]{2,1,0:T(2,128)(2,1)S(1)}, u32[]{:S(2)}, u32[]{:S(2)}) collective-permute-start(bf16[64,1,128]{2,1,0:T(2,128)(2,1)S(1)} %get-tuple-element.55), channel_id=1, source_target_pairs={{4,0},{8,4},{12,8},{5,1},{9,5},{13,9},{6,2},{10,6},{14,10},{7,3},{... | collective-permute-start | bytes 49160 | tf_op jit(solution)/shard_map/ppermute | solution.py:22
  92.3 82.5 %all-reduce.6.cloned.1.call-start = ((), (), s32[]{:S(2)}) async-start(), calls=%async_computation.2 | async-start | bytes 589824 | tf_op jit(solution)/shard_map/psum | solution.py:7
  94.2 4.4 %collective-permute-start.11 = (bf16[64,10,1]{2,0,1:T(8,128)(2,1)S(1)}, bf16[64,10,1]{2,0,1:T(8,128)(2,1)S(1)}, u32[]{:S(2)}, u32[]{:S(2)}) collective-permute-start(bf16[64,10,1]{2,0,1:T(8,128)(2,1)S(1)} %get-tuple-element.52), channel_id=1, source_target_pairs={{1,0},{2,1},{3,2},{5,4},{6,5},{7,6},{9,8},{10,9},{11,10},{13,12},{... | collective-permute-start | bytes 3848 | tf_op jit(solution)/shard_map/ppermute | solution.py:22
  95.5 4.2 %collective-permute-start.10 = (bf16[64,10,1]{2,0,1:T(8,128)(2,1)S(1)}, bf16[64,10,1]{2,0,1:T(8,128)(2,1)S(1)}, u32[]{:S(2)}, u32[]{:S(2)}) collective-permute-start(bf16[64,10,1]{2,0,1:T(8,128)(2,1)S(1)} %get-tuple-element.51), channel_id=1, source_target_pairs={{0,1},{1,2},{2,3},{4,5},{5,6},{6,7},{8,9},{9,10},{10,11},{12,13},{... | collective-permute-start | bytes 3848 | tf_op jit(solution)/shard_map/ppermute | solution.py:20
Sparse Core Ops, SparseCore 0:
  64.5 20.1 reduce-scatter.1
  92.4 43.9 all-reduce.7
  138.8 35.9 all-reduce.5
